TPU v7x, 32 devices: a whole 2x2x4 slice. The times are simulated.
32 devices in a mesh: groups: 2 (over y), ctx: 4 (over x, core), tp: 4 (over z).
Axes of the slice: x: 2, y: 2, z: 4, core: 2. Of those that a mesh axis runs over, the one named last changes fastest.
Arguments:
- queries: bfloat16 [2048, 4096], P(('groups', 'ctx'), 'tp'), parts along dimension 0, as said below
- keys: bfloat16 [2048, 1024], P(('groups', 'ctx'), 'tp'), parts along dimension 0, as said below
- values: bfloat16 [2048, 1024], P(('groups', 'ctx'), 'tp'), parts along dimension 0, may hold values from -24 to 24
- teacher_residual: bfloat16 [2048, 8192], P(('groups', 'ctx'), 'tp'), parts along dimension 0, as said below
- teacher_out: bfloat16 [4096, 8192], P('tp', 'ctx'), may hold values from -0.09375 to 0.09375
- teacher_gain: float32 [8192], replicated, may hold values from 0.1 to 1.9
- projector: bfloat16 [8192, 3072], P('tp'), may hold values from -0.0625 to 0.0625
- span_starts: int32 [2048], P(('groups', 'ctx')), parts along dimension 0, may hold values from 0 to 1023, as said below
- span_ends: int32 [2048], P(('groups', 'ctx')), parts along dimension 0, may hold values from 1 to 1024, as said below
- aligned_counts: int32 [8], P(('groups', 'ctx')), parts along dimension 0, may hold values from 128 to 256, as said below
- student_context: bfloat16 [2048, 3072], P(('groups', 'ctx'), 'tp'), parts along dimension 0, may hold values from -0.75 to 0.75
- student_out: bfloat16 [3072, 3072], P('tp'), may hold values from -0.109375 to 0.109375
- student_residual: bfloat16 [2048, 3072], P(('groups', 'ctx'), 'tp'), parts along dimension 0, may hold values from -1.5 to 1.5
Outputs:
- grad_out: float32 [6144, 3072], P(('groups', 'tp'), 'ctx'), parts along dimension 0
- grad_context: bfloat16 [2048, 3072], P(('groups', 'ctx'), 'tp'), parts along dimension 0
There are 2 independent parts, one for each index of `groups`. A program takes and returns all parts, laid end to end along the dimension named above; an argument that names none is the same for every part. Nothing has to cross between parts.
Inputs may be any that keep to these rules, and one draw needn't show every extreme that they name: `queries`: entries lie within -12 to 12. `keys`: entries lie within -12 to 12. `teacher_residual`: entries lie within -8 to 8. Student token s takes teacher rows span_starts[s] to span_ends[s] - 1; span_starts[s] lies in s - 16 .. s (never below 0), and the first token of every shard of 256 tokens starts exactly 16 rows back where the sequence allows. span_ends[s] lies in s + 1 .. s + 1 + 16 (never above 1024); the last token of every shard of 256 tokens ends exactly 16 rows ahead where the sequence allows. Shard j's first aligned_counts[j] tokens are distilled, its later ones are not.
All inputs are finite; a program needn't handle non-finite values.
Results may differ from a plain program's by a relative error of at most 0.017.
Values may be sent and summed in bfloat16 or wider, within the bound.
A program may use at most 128 MiB of HBM per device.

v0:
```python
import math

import jax
import jax.numpy as jnp
from jax import lax
from jax.sharding import PartitionSpec as P

TD = 8192
HEADS = 32
KV_HEADS = 8
HEAD = 128
HALO = 16


def padded(cells, sides, width):
    for axis, dim in sides:
        count = lax.axis_size(axis)
        ends = count - 1
        head = lax.slice_in_dim(cells, 0, width, axis=dim)
        tail = lax.slice_in_dim(cells, cells.shape[dim] - width, cells.shape[dim], axis=dim)
        cells = jnp.concatenate(
            [
                lax.ppermute(tail, axis, [(i, (i + 1) % count) for i in range(ends)]),
                cells,
                lax.ppermute(head, axis, [((i + 1) % count, i) for i in range(ends)]),
            ],
            axis=dim,
        )
    return cells


def attend_local(queries, keys, values):
    row_count = queries.shape[0]
    key_heads = keys.shape[1] // HEAD
    per_key = HEADS // KV_HEADS
    score_scale = 1.0 / math.sqrt(HEAD)
    query_grid = queries.reshape(row_count, key_heads, per_key, HEAD)
    query_position = lax.axis_index("ctx") * row_count + jnp.arange(row_count, dtype=jnp.int32)
    row_max = jnp.full((key_heads, per_key, row_count), -1e30, jnp.float32)
    key_piece = lax.all_gather(keys, "ctx", axis=0, tiled=True)
    value_piece = lax.all_gather(values, "ctx", axis=0, tiled=True)
    piece_rows = key_piece.shape[0]
    key_grid = key_piece.reshape(piece_rows, key_heads, HEAD)
    value_grid = value_piece.reshape(piece_rows, key_heads, HEAD)
    scores = (
        jnp.einsum("qkgd,ckd->kgqc", query_grid, key_grid, preferred_element_type=jnp.float32)
        * score_scale
    )
    key_position = jnp.arange(piece_rows, dtype=jnp.int32)
    allowed = key_position[None, :] <= query_position[:, None]
    scores = jnp.where(allowed, scores, -jnp.inf)
    new_max = jnp.maximum(row_max, jnp.max(scores, axis=3))
    exponent = jnp.exp(scores - new_max[..., None])
    row_total = jnp.sum(exponent, axis=3)
    mixed_values = jnp.einsum(
        "kgqc,ckd->kgqd",
        exponent.astype(jnp.bfloat16),
        value_grid,
        preferred_element_type=jnp.float32,
    )
    weighted = mixed_values
    row_max, row_total, weighted = (new_max, row_total, weighted)
    attended = (weighted / row_total[..., None]).astype(jnp.bfloat16)
    return jnp.transpose(attended, (2, 0, 1, 3)).reshape(row_count, key_heads * per_key * HEAD)


def body(
    queries,
    keys,
    values,
    teacher_residual,
    teacher_out,
    teacher_gain,
    projector,
    span_starts,
    span_ends,
    aligned_counts,
    student_context,
    student_out,
    student_residual,
):
    attended = attend_local(queries, keys, values)
    row_count = attended.shape[0]
    feature_width = teacher_residual.shape[1]
    column_terms = jnp.dot(
        attended,
        lax.all_gather(teacher_out, "ctx", axis=1, tiled=True),
        preferred_element_type=jnp.float32,
    )
    summed = lax.psum_scatter(
        column_terms.astype(jnp.bfloat16), "tp", scatter_dimension=1, tiled=True
    ).astype(jnp.float32)
    hidden = teacher_residual.astype(jnp.float32) + summed
    squares = lax.psum(jnp.sum(hidden * hidden, axis=1), "tp")
    gain_share = lax.dynamic_slice_in_dim(
        teacher_gain, lax.axis_index("tp") * feature_width, feature_width, 0
    )
    normed = (hidden * lax.rsqrt(squares[:, None] / TD + 1e-06) * gain_share).astype(jnp.bfloat16)
    extended = padded(normed, (("ctx", 0),), HALO)
    teacher_position = (
        lax.axis_index("ctx") * row_count - HALO + jnp.arange(row_count + 2 * HALO, dtype=jnp.int32)
    )
    inside = (teacher_position[None, :] >= span_starts[:, None]) & (
        teacher_position[None, :] < span_ends[:, None]
    )
    span_sums = jnp.dot(inside.astype(jnp.bfloat16), extended, preferred_element_type=jnp.float32)
    lengths = (span_ends - span_starts).astype(jnp.float32)
    pooled = (span_sums / lengths[:, None]).astype(jnp.bfloat16)
    student_term = jnp.dot(student_context, student_out, preferred_element_type=jnp.float32)
    target_term = jnp.dot(pooled, projector, preferred_element_type=jnp.float32)
    student_share, target_share = (
        lax.psum_scatter(
            student_term.astype(jnp.bfloat16), "tp", scatter_dimension=1, tiled=True
        ).astype(jnp.float32),
        lax.psum_scatter(
            target_term.astype(jnp.bfloat16), "tp", scatter_dimension=1, tiled=True
        ).astype(jnp.float32),
    )
    residual_gap = student_share - target_share
    local_rows = jnp.arange(row_count, dtype=jnp.int32)
    valid_rows = local_rows < aligned_counts[0]
    grad_hidden = jnp.where(
        valid_rows[:, None], student_residual.astype(jnp.float32) + residual_gap, 0.0
    ).astype(jnp.bfloat16)
    grad_full = lax.all_gather(grad_hidden, "tp", axis=1, tiled=True)
    grad_context = lax.dot_general(
        grad_full, student_out, (((1,), (1,)), ((), ())), preferred_element_type=jnp.float32
    ).astype(jnp.bfloat16)
    grad_terms = lax.dot_general(
        student_context, grad_full, (((0,), (0,)), ((), ())), preferred_element_type=jnp.float32
    )
    grad_out = lax.psum_scatter(
        grad_terms.astype(jnp.bfloat16), "ctx", scatter_dimension=1, tiled=True
    ).astype(jnp.float32)
    return (grad_out, grad_context)


def solution(mesh):
    return jax.shard_map(
        body,
        mesh=mesh,
        in_specs=(
            P(("groups", "ctx"), "tp"),
            P(("groups", "ctx"), "tp"),
            P(("groups", "ctx"), "tp"),
            P(("groups", "ctx"), "tp"),
            P("tp", "ctx"),
            P(),
            P("tp", None),
            P(("groups", "ctx")),
            P(("groups", "ctx")),
            P(("groups", "ctx")),
            P(("groups", "ctx"), "tp"),
            P("tp", None),
            P(("groups", "ctx"), "tp"),
        ),
        out_specs=(P(("groups", "tp"), "ctx"), P(("groups", "ctx"), "tp")),
        check_vma=False,
    )
```

profile of v0, /device:TPU:0, one launch (start us, length us, event | category | flops | bytes accessed | tf_op | source)
XLA Modules:
  0.0 382.4 jit_solution(6342919857602728855)
XLA Ops:
  8.7 8.6 %all_gather.13 = bf16[1024,256]{1,0:T(8,128)(2,1)S(1)} all-gather(bf16[256,256]{1,0:T(8,128)(2,1)S(1)} %copy-done.5), channel_id=1, replica_groups=mesh['groups'=2,'ctx'=4,'tp'=4] {'ctx'}, dimensions={0}, use_global_device_ids=true | all-gather | bytes 655360 | tf_op jit(solution)/shard_map/all_gather | solution.py:41
  17.6 7.3 %all_gather.12 = bf16[1024,256]{0,1:T(8,128)(2,1)S(1)} all-gather(bf16[256,256]{0,1:T(8,128)(2,1)S(1)} %copy.19), channel_id=1, replica_groups=mesh['groups'=2,'ctx'=4,'tp'=4] {'ctx'}, dimensions={0}, use_global_device_ids=true | all-gather | bytes 655360 | tf_op jit(solution)/shard_map/all_gather | solution.py:40
  25.0 1.5 fusion.2
  26.6 1.7 fusion
  28.3 2.3 divide_convert_fusion
  30.6 87.7 %all-gather.3.cloned.1.call-done = bf16[1024,8192]{1,0:T(8,128)(2,1)} async-done(((bf16[1024,2048]{1,0:T(8,128)(2,1)}), bf16[1024,8192]{1,0:T(8,128)(2,1)}) %all-gather.3.cloned.1.call-update) | async-done | bytes 16777232 | tf_op jit(solution)/shard_map/all_gather | solution.py:87
  118.3 12.0 %convolution_convert_fusion = bf16[256,8192]{1,0:T(8,128)(2,1)} fusion(bf16[256,1024]{0,1:T(8,128)(2,1)S(1)} %bitcast.46, bf16[1024,8192]{1,0:T(8,128)(2,1)} %all-gather.3.cloned.1.call-done), kind=kOutput, calls=%fused_computation | convolution fusion | flops 4297064448 | bytes 21495808 | tf_op jit(solution)/shard_map/dot_general | solution.py:85
  130.4 5.0 %convolution_convert_fusion.2 = bf16[256,3072]{1,0:T(8,128)(2,1)} fusion(bf16[256,768]{1,0:T(8,128)(2,1)S(1)} %copy-done, bf16[768,3072]{1,0:T(8,128)(2,1)} %param.24), kind=kOutput, calls=%fused_computation.10 | convolution fusion | flops 1208745984 | bytes 6684672 | tf_op jit(solution)/shard_map/dot_general | solution.py:109
  136.2 71.1 %reduce-scatter.7.cloned.1.call-done = bf16[256,2048]{1,0:T(8,128)(2,1)} async-done(((bf16[256,8192]{1,0:T(8,128)(2,1)}), bf16[256,2048]{1,0:T(8,128)(2,1)}) %reduce-scatter.7.cloned.1.call-update) | async-done | bytes 1048592 | tf_op jit(solution)/shard_map/reduce_scatter | solution.py:90
  207.2 1.6 multiply_reduce_fusion
  208.9 11.0 %psum.7 = f32[256]{0:T(256)S(1)} all-reduce(f32[256]{0:T(256)S(1)} %multiply_reduce_fusion), channel_id=1, replica_groups=mesh['groups'=2,'ctx'=4,'tp'=4] {'tp'}, use_global_device_ids=true, to_apply=%region_5.6 | all-reduce | flops 256 | bytes 2048 | tf_op jit(solution)/shard_map/psum | solution.py:94
  219.9 1.7 multiply_convert_fusion
  221.7 1.5 collective-permute-start
  224.5 3.8 collective-permute-done.1
  228.3 9.8 %convolution_convert_fusion.3 = bf16[256,3072]{1,0:T(8,128)(2,1)} fusion(bf16[2048,3072]{1,0:T(8,128)(2,1)} %param.19, bf16[16,2048]{1,0:T(8,128)(2,1)S(1)} %collective-permute-done.1, bf16[256,2048]{1,0:T(8,128)(2,1)S(1)} %multiply_convert_fusion, bf16[16,2048]{1,0:T(8,128)(2,1)S(1)} %collective-permute-done, f32[256]{0:T(256)S(1)} %subtract_convert_fusion, ...), kind=kOutput, calls=%fused_computation.11 | convolution fusion | flops 3528810496 | bytes 15339648 | tf_op jit(solution)/shard_map/dot_general | solution.py:110
  238.8 6.7 %reduce-scatter.5.cloned.1.call-done = bf16[256,768]{1,0:T(8,128)(2,1)} async-done(((bf16[256,3072]{1,0:T(8,128)(2,1)}), bf16[256,768]{1,0:T(8,128)(2,1)}) %reduce-scatter.5.cloned.1.call-update) | async-done | bytes 393232 | tf_op jit(solution)/shard_map/reduce_scatter | solution.py:112
  245.5 37.2 %reduce-scatter.9.cloned.1.call-done = bf16[256,768]{1,0:T(8,128)(2,1)} async-done(((bf16[256,3072]{1,0:T(8,128)(2,1)}), bf16[256,768]{1,0:T(8,128)(2,1)}) %reduce-scatter.9.cloned.1.call-update) | async-done | bytes 393232 | tf_op jit(solution)/shard_map/reduce_scatter | solution.py:115
  282.6 2.0 select_convert_fusion
  284.8 36.2 %all-gather.5.cloned.1.call-done = bf16[256,3072]{1,0:T(8,128)(2,1)} async-done(((bf16[256,768]{1,0:T(8,128)(2,1)}), bf16[256,3072]{1,0:T(8,128)(2,1)}) %all-gather.5.cloned.1.call-update) | async-done | bytes 1572880 | tf_op jit(solution)/shard_map/all_gather | solution.py:125
  321.0 5.0 %fusion.3 = bf16[768,3072]{0,1:T(8,128)(2,1)} fusion(bf16[256,3072]{1,0:T(8,128)(2,1)} %all-gather.5.cloned.1.call-done, bf16[256,768]{1,0:T(8,128)(2,1)S(1)} %copy-done), kind=kOutput, calls=%fused_computation.7 | convolution fusion | flops 1210318848 | bytes 6684672 | tf_op jit(solution)/shard_map/dot_general | solution.py:129
  326.0 1.4 copy-done.2
  327.4 4.5 %convolution_convert_fusion.4 = bf16[256,768]{1,0:T(8,128)(2,1)} fusion(bf16[256,3072]{1,0:T(8,128)(2,1)S(1)} %copy-done.2, bf16[768,3072]{1,0:T(8,128)(2,1)} %param.24), kind=kOutput, calls=%fused_computation.18 | convolution fusion | flops 1208156160 | bytes 6684672 | tf_op jit(solution)/shard_map/dot_general | solution.py:126
  331.9 41.0 %reduce-scatter.11.cloned.1.call-done = bf16[768,768]{0,1:T(8,128)(2,1)} async-done(((bf16[768,3072]{0,1:T(8,128)(2,1)}), bf16[768,768]{0,1:T(8,128)(2,1)}) %reduce-scatter.11.cloned.1.call-update) | async-done | bytes 1179664 | tf_op jit(solution)/shard_map/reduce_scatter | solution.py:132
  372.9 2.7 copy.24
  (43 shorter events, 4.2 us)
Async XLA Ops:
  7.2 123.2 %copy-start = (bf16[256,768]{1,0:T(8,128)(2,1)S(1)}, bf16[256,768]{1,0:T(8,128)(2,1)}, u32[]{:S(2)}) copy-start(bf16[256,768]{1,0:T(8,128)(2,1)} %param.23) | copy-start | bytes 1179652
  7.2 1.0 copy-start.6
  7.2 1.1 copy-start.3
  7.2 1.5 copy-start.5
  7.2 111.0 %all-gather.3.cloned.1.call-start = ((), (), s32[]{:S(2)}) async-start(), calls=%async_computation.5 | async-start | bytes 20971520 | tf_op jit(solution)/shard_map/all_gather | solution.py:87
  7.9 199.3 %reduce-scatter.7.cloned.1.call-start = ((), (), s32[]{:S(2)}) async-start(), calls=%async_computation.6 | async-start | bytes 5242880 | tf_op jit(solution)/shard_map/reduce_scatter | solution.py:90
  130.3 5.8 %copy-start.7 = (s32[256]{0:T(256)S(1)}, s32[256]{0:T(256)}, u32[]{:S(2)}) copy-start(s32[256]{0:T(256)} %param.21) | copy-start | bytes 3076
  130.3 5.8 %copy-start.8 = (s32[256]{0:T(256)S(1)}, s32[256]{0:T(256)}, u32[]{:S(2)}) copy-start(s32[256]{0:T(256)} %param.20) | copy-start | bytes 3076
  130.3 76.9 %copy-start.1 = (bf16[256,2048]{1,0:T(8,128)(2,1)S(1)}, bf16[256,2048]{1,0:T(8,128)(2,1)}, u32[]{:S(2)}) copy-start(bf16[256,2048]{1,0:T(8,128)(2,1)} %param.16) | copy-start | bytes 3145732
  130.4 115.1 %reduce-scatter.5.cloned.1.call-start = ((), (), s32[]{:S(2)}) async-start(), calls=%async_computation.4 | async-start | bytes 1966080 | tf_op jit(solution)/shard_map/reduce_scatter | solution.py:112
  135.4 147.3 %reduce-scatter.9.cloned.1.call-start = ((), (), s32[]{:S(2)}) async-start(), calls=%async_computation.7 | async-start | bytes 1966080 | tf_op jit(solution)/shard_map/reduce_scatter | solution.py:115
  221.7 2.8 collective-permute-start
  223.1 5.1 %collective-permute-start.1 = (bf16[16,2048]{1,0:T(8,128)(2,1)S(1)}, bf16[16,2048]{1,0:T(8,128)(2,1)S(1)}, u32[]{:S(2)}, u32[]{:S(2)}) collective-permute-start(bf16[16,2048]{1,0:T(8,128)(2,1)S(1)} %get-tuple-element.7), channel_id=1, source_target_pairs={{4,0},{8,4},{12,8},{5,1},{9,5},{13,9},{6,2},{10,6},{14,10},{7,3},{... | collective-permute-start | bytes 196616 | tf_op jit(solution)/shard_map/ppermute | solution.py:25
  224.4 58.2 %copy-start.4 = (bf16[256,768]{1,0:T(8,128)(2,1)S(1)}, bf16[256,768]{1,0:T(8,128)(2,1)}, u32[]{:S(2)}) copy-start(bf16[256,768]{1,0:T(8,128)(2,1)} %param.25) | copy-start | bytes 1179652
  238.1 82.9 %all-gather.5.cloned.1.call-start = ((), (), s32[]{:S(2)}) async-start(), calls=%async_computation.8 | async-start | bytes 1966080 | tf_op jit(solution)/shard_map/all_gather | solution.py:125
  284.7 88.1 %reduce-scatter.11.cloned.1.call-start = ((), (), s32[]{:S(2)}) async-start(), calls=%async_computation.9 | async-start | bytes 5898240 | tf_op jit(solution)/shard_map/reduce_scatter | solution.py:132
  326.0 1.4 copy-start.2
Sparse Core Ops, SparseCore 0:
  9.6 108.6 all-gather.2
  130.4 76.7 reduce-scatter.6
  209.7 35.7 reduce-scatter.4
  248.3 34.2 reduce-scatter.8
  284.8 36.0 all-gather.4
  326.1 46.7 reduce-scatter.10
where the time goes:
time: 383 us; the launch traced here: 382 us
  waiting for transfers between devices  284 us (74%)
  matrix products  40.1 us (10%)
  blocking collectives  27 us (7%)
  between operations  15 us (4%)
  other arithmetic  7.3 us (2%)
  local copies, waits for them, and re-layouts  5.75 us (2%)
    all_gather x1, waiting for transfers between devices, body(): lax.all_gather(teacher_out, 'ctx', axis=1, tiled=True)  87.7 us
    reduce_scatter x1, waiting for transfers between devices, body(): lax.psum_scatter(column_terms.astype(jnp.bfloat16), 'tp', scatter_dimensi...  71.1 us
    reduce_scatter x1, waiting for transfers between devices, body(): lax.psum_scatter(grad_terms.astype(jnp.bfloat16), 'ctx', scatter_dimensio...  41 us
    reduce_scatter x1, waiting for transfers between devices, body(): lax.psum_scatter(target_term.astype(jnp.bfloat16), 'tp', scatter_dimensio...  37.2 us
    all_gather x1, waiting for transfers between devices, body(): grad_full = lax.all_gather(grad_hidden, 'tp', axis=1, tiled=True)  36.2 us
    dot_general x1, matrix products, body(): jnp.dot(attended, lax.all_gather(teacher_out, 'ctx', axis=1, tiled=True),...  12 us
    psum x1, blocking collectives, body(): squares = lax.psum(jnp.sum(hidden * hidden, axis=1), 'tp')  11 us
    dot_general x1, matrix products, body(): target_term = jnp.dot(pooled, projector, preferred_element_type=jnp.float32)  9.79 us
  transfers between devices with their start and end apart: 8, of which 7 were waited for; matrix products, arithmetic and copies ran while one was open for 8% of the time, Pallas kernels for 0%

commit v1 on v0

--- a/solution.py
+++ b/solution.py
@@ -108,15 +108,9 @@
     pooled = (span_sums / lengths[:, None]).astype(jnp.bfloat16)
     student_term = jnp.dot(student_context, student_out, preferred_element_type=jnp.float32)
     target_term = jnp.dot(pooled, projector, preferred_element_type=jnp.float32)
-    student_share, target_share = (
-        lax.psum_scatter(
-            student_term.astype(jnp.bfloat16), "tp", scatter_dimension=1, tiled=True
-        ).astype(jnp.float32),
-        lax.psum_scatter(
-            target_term.astype(jnp.bfloat16), "tp", scatter_dimension=1, tiled=True
-        ).astype(jnp.float32),
-    )
-    residual_gap = student_share - target_share
+    residual_gap = lax.psum_scatter(
+        (student_term - target_term).astype(jnp.bfloat16), "tp", scatter_dimension=1, tiled=True
+    ).astype(jnp.float32)
     local_rows = jnp.arange(row_count, dtype=jnp.int32)
     valid_rows = local_rows < aligned_counts[0]
     grad_hidden = jnp.where(
@@ -126,12 +120,11 @@
     grad_context = lax.dot_general(
         grad_full, student_out, (((1,), (1,)), ((), ())), preferred_element_type=jnp.float32
     ).astype(jnp.bfloat16)
-    grad_terms = lax.dot_general(
-        student_context, grad_full, (((0,), (0,)), ((), ())), preferred_element_type=jnp.float32
+    context_rows = lax.all_gather(student_context, "ctx", axis=0, tiled=True)
+    grad_columns = lax.all_to_all(grad_full, "ctx", split_axis=1, concat_axis=0, tiled=True)
+    grad_out = lax.dot_general(
+        context_rows, grad_columns, (((0,), (0,)), ((), ())), preferred_element_type=jnp.float32
     )
-    grad_out = lax.psum_scatter(
-        grad_terms.astype(jnp.bfloat16), "ctx", scatter_dimension=1, tiled=True
-    ).astype(jnp.float32)
     return (grad_out, grad_context)
 
 

time: 383 us -> 366 us (0.956)
  waiting for transfers between devices: 284 us -> 262 us
    reduce_scatter x3 -> x1, waiting for transfers between devices: 84.8 us -> 34.6 us  [body(): lax.psum_scatter((student_term - target_term).astype(jnp.bfloat16), 'tp',...]
    all_gather x0 -> x1, waiting for transfers between devices: none -> 17.1 us  [body(): context_rows = lax.all_gather(student_context, 'ctx', axis=0, tiled=True)]
    all_to_all x0 -> x1, waiting for transfers between devices: none -> 6.45 us  [body(): lax.all_to_all(grad_full, 'ctx', split_axis=1, concat_axis=0, tiled=True)]
    reduce_scatter x1, waiting for transfers between devices: 71.1 us -> 76.1 us  [body(): lax.psum_scatter(column_terms.astype(jnp.bfloat16), 'tp', scatter_dimensi...]
  transfers between devices with their start and end apart: 8 -> 8, of which waited for: 7 -> 7; matrix products, arithmetic and copies ran while one was open for 8% -> 4% of each run, Pallas kernels for 0% -> 0%
where the time goes in v1:
time: 366 us; the launch traced here: 365 us
  waiting for transfers between devices  262 us (72%)
  matrix products  40.2 us (11%)
  blocking collectives  26.9 us (7%)
  between operations  14.6 us (4%)
  local copies, waits for them, and re-layouts  7.55 us (2%)
  other arithmetic  7.15 us (2%)
  starting transfers between devices  6.53 us (2%)
    all_gather x1, waiting for transfers between devices, body(): lax.all_gather(teacher_out, 'ctx', axis=1, tiled=True)  87.7 us
    reduce_scatter x1, waiting for transfers between devices, body(): lax.psum_scatter(column_terms.astype(jnp.bfloat16), 'tp', scatter_dimensi...  76.1 us
    all_gather x1, waiting for transfers between devices, body(): grad_full = lax.all_gather(grad_hidden, 'tp', axis=1, tiled=True)  35.7 us
    reduce_scatter x1, waiting for transfers between devices, body(): lax.psum_scatter((student_term - target_term).astype(jnp.bfloat16), 'tp',...  34.6 us
    all_gather x1, waiting for transfers between devices, body(): context_rows = lax.all_gather(student_context, 'ctx', axis=0, tiled=True)  17.1 us
    dot_general x1, matrix products, body(): jnp.dot(attended, lax.all_gather(teacher_out, 'ctx', axis=1, tiled=True),...  12 us
    psum x1, blocking collectives, body(): squares = lax.psum(jnp.sum(hidden * hidden, axis=1), 'tp')  10.9 us
    dot_general x1, matrix products, body(): target_term = jnp.dot(pooled, projector, preferred_element_type=jnp.float32)  10.2 us
  transfers between devices with their start and end apart: 8, of which 7 were waited for; matrix products, arithmetic and copies ran while one was open for 4% of the time, Pallas kernels for 0%

profile of v1, /device:TPU:0, one launch (start us, length us, event | category | flops | bytes accessed | tf_op | source)
XLA Modules:
  0.0 365.3 jit_solution(15759481534300824340)
XLA Ops:
  8.7 8.6 %all_gather.16 = bf16[1024,256]{1,0:T(8,128)(2,1)S(1)} all-gather(bf16[256,256]{1,0:T(8,128)(2,1)S(1)} %copy-done.6), channel_id=1, replica_groups=mesh['groups'=2,'ctx'=4,'tp'=4] {'ctx'}, dimensions={0}, use_global_device_ids=true | all-gather | bytes 655360 | tf_op jit(solution)/shard_map/all_gather | solution.py:41
  17.5 7.3 %all_gather.15 = bf16[1024,256]{0,1:T(8,128)(2,1)S(1)} all-gather(bf16[256,256]{0,1:T(8,128)(2,1)S(1)} %copy.19), channel_id=1, replica_groups=mesh['groups'=2,'ctx'=4,'tp'=4] {'ctx'}, dimensions={0}, use_global_device_ids=true | all-gather | bytes 655360 | tf_op jit(solution)/shard_map/all_gather | solution.py:40
  25.0 1.5 fusion.2
  26.6 1.7 fusion
  28.3 2.3 divide_convert_fusion
  30.5 87.7 %all-gather.4.cloned.1.call-done = bf16[1024,8192]{1,0:T(8,128)(2,1)} async-done(((bf16[1024,2048]{1,0:T(8,128)(2,1)}), bf16[1024,8192]{1,0:T(8,128)(2,1)}) %all-gather.4.cloned.1.call-update) | async-done | bytes 16777232 | tf_op jit(solution)/shard_map/all_gather | solution.py:87
  118.2 12.0 %convolution_convert_fusion = bf16[256,8192]{1,0:T(8,128)(2,1)} fusion(bf16[256,1024]{0,1:T(8,128)(2,1)S(1)} %bitcast.55, bf16[1024,8192]{1,0:T(8,128)(2,1)} %all-gather.4.cloned.1.call-done), kind=kOutput, calls=%fused_computation | convolution fusion | flops 4297064448 | bytes 21495808 | tf_op jit(solution)/shard_map/dot_general | solution.py:85
  131.2 76.1 %reduce-scatter.3.cloned.1.call-done = bf16[256,2048]{1,0:T(8,128)(2,1)} async-done(((bf16[256,8192]{1,0:T(8,128)(2,1)}), bf16[256,2048]{1,0:T(8,128)(2,1)}) %reduce-scatter.3.cloned.1.call-update) | async-done | bytes 1048592 | tf_op jit(solution)/shard_map/reduce_scatter | solution.py:90
  207.2 1.6 multiply_reduce_fusion
  208.9 10.9 %psum.7 = f32[256]{0:T(256)S(1)} all-reduce(f32[256]{0:T(256)S(1)} %multiply_reduce_fusion), channel_id=1, replica_groups=mesh['groups'=2,'ctx'=4,'tp'=4] {'tp'}, use_global_device_ids=true, to_apply=%region_4.5 | all-reduce | flops 256 | bytes 2048 | tf_op jit(solution)/shard_map/psum | solution.py:94
  219.8 1.7 multiply_convert_fusion
  224.4 3.6 collective-permute-done.1
  228.0 10.2 %fusion.11 = f32[256,3072]{1,0:T(8,128)} fusion(bf16[2048,3072]{1,0:T(8,128)(2,1)} %param.19, bf16[16,2048]{1,0:T(8,128)(2,1)S(1)} %collective-permute-done.1, bf16[256,2048]{1,0:T(8,128)(2,1)S(1)} %multiply_convert_fusion, bf16[16,2048]{1,0:T(8,128)(2,1)S(1)} %collective-permute-done, f32[256]{0:T(256)S(1)} %subtract_convert_fusion, ...), kind=kOutput, calls=%fused_computation.19 | convolution fusion | flops 3528024064 | bytes 16912512 | tf_op jit(solution)/shard_map/dot_general | solution.py:110
  238.2 5.9 %fusion.6 = bf16[256,3072]{1,0:T(8,128)(2,1)} fusion(f32[256,3072]{1,0:T(8,128)} %fusion.11, bf16[256,768]{1,0:T(8,128)(2,1)S(1)} %copy-done.4, bf16[768,3072]{1,0:T(8,128)(2,1)} %param.24), kind=kOutput, calls=%fused_computation.9 | convolution fusion | flops 1209532416 | bytes 9830400 | tf_op jit(solution)/shard_map/dot_general | solution.py:109
  244.8 34.6 %reduce-scatter.5.cloned.1.call-done = bf16[256,768]{1,0:T(8,128)(2,1)} async-done(((bf16[256,3072]{1,0:T(8,128)(2,1)}), bf16[256,768]{1,0:T(8,128)(2,1)}) %reduce-scatter.5.cloned.1.call-update) | async-done | bytes 393232 | tf_op jit(solution)/shard_map/reduce_scatter | solution.py:111
  279.4 1.9 select_convert_fusion
  281.9 35.7 %all-gather.6.cloned.1.call-done = bf16[256,3072]{1,0:T(8,128)(2,1)} async-done(((bf16[256,768]{1,0:T(8,128)(2,1)}), bf16[256,3072]{1,0:T(8,128)(2,1)}) %all-gather.6.cloned.1.call-update) | async-done | bytes 1572880 | tf_op jit(solution)/shard_map/all_gather | solution.py:119
  317.5 2.8 copy.37
  320.3 3.6 all-to-all-start
  323.9 4.9 %convolution_convert_fusion.1 = bf16[256,768]{1,0:T(8,128)(2,1)} fusion(bf16[256,3072]{1,0:T(8,128)(2,1)S(1)} %copy-done.1, bf16[768,3072]{1,0:T(8,128)(2,1)} %param.24), kind=kOutput, calls=%fused_computation.18 | convolution fusion | flops 1208156160 | bytes 6684672 | tf_op jit(solution)/shard_map/dot_general | solution.py:120
  328.8 17.1 %all-gather.8.cloned.1.call-done = bf16[1024,768]{1,0:T(8,128)(2,1)} async-done(((bf16[256,768]{1,0:T(8,128)(2,1)}), bf16[1024,768]{1,0:T(8,128)(2,1)}) %all-gather.8.cloned.1.call-update) | async-done | bytes 1572880 | tf_op jit(solution)/shard_map/all_gather | solution.py:123
  345.9 6.4 %all-to-all-done = bf16[256,4,768]{2,0,1:T(8,128)(2,1)S(1)} async-done(((bf16[256,4,768]{2,0,1:T(8,128)(2,1)}), bf16[256,4,768]{2,0,1:T(8,128)(2,1)S(1)}, u32[]{:S(2)}, u32[]{:S(2)}) %all-to-all-start) | async-done | bytes 1572896 | tf_op jit(solution)/shard_map/all_to_all | solution.py:124
  353.5 3.3 convolution_bitcast_fusion
  356.8 2.0 copy.25
  (45 shorter events, 7.3 us)
Async XLA Ops:
  7.2 0.9 copy-start.7
  7.2 1.1 copy-start.3
  7.2 1.5 copy-start.6
  7.2 111.0 %all-gather.4.cloned.1.call-start = ((), (), s32[]{:S(2)}) async-start(), calls=%async_computation.3 | async-start | bytes 20971520 | tf_op jit(solution)/shard_map/all_gather | solution.py:87
  7.9 199.3 %reduce-scatter.3.cloned.1.call-start = ((), (), s32[]{:S(2)}) async-start(), calls=%async_computation.4 | async-start | bytes 5242880 | tf_op jit(solution)/shard_map/reduce_scatter | solution.py:90
  130.3 0.9 copy-start.8
  130.3 0.9 copy-start.9
  130.3 77.0 %copy-start = (bf16[256,2048]{1,0:T(8,128)(2,1)S(1)}, bf16[256,2048]{1,0:T(8,128)(2,1)}, u32[]{:S(2)}) copy-start(bf16[256,2048]{1,0:T(8,128)(2,1)} %param.16) | copy-start | bytes 3145732
  130.3 149.1 %reduce-scatter.5.cloned.1.call-start = ((), (), s32[]{:S(2)}) async-start(), calls=%async_computation.5 | async-start | bytes 1966080 | tf_op jit(solution)/shard_map/reduce_scatter | solution.py:111
  221.6 2.8 collective-permute-start
  222.9 5.1 %collective-permute-start.1 = (bf16[16,2048]{1,0:T(8,128)(2,1)S(1)}, bf16[16,2048]{1,0:T(8,128)(2,1)S(1)}, u32[]{:S(2)}, u32[]{:S(2)}) collective-permute-start(bf16[16,2048]{1,0:T(8,128)(2,1)S(1)} %get-tuple-element.7), channel_id=1, source_target_pairs={{4,0},{8,4},{12,8},{5,1},{9,5},{13,9},{6,2},{10,6},{14,10},{7,3},{... | collective-permute-start | bytes 196616 | tf_op jit(solution)/shard_map/ppermute | solution.py:25
  224.4 13.8 %copy-start.4 = (bf16[256,768]{1,0:T(8,128)(2,1)S(1)}, bf16[256,768]{1,0:T(8,128)(2,1)}, u32[]{:S(2)}) copy-start(bf16[256,768]{1,0:T(8,128)(2,1)} %param.23) | copy-start | bytes 1179652
  238.2 41.2 %copy-start.5 = (bf16[256,768]{1,0:T(8,128)(2,1)S(1)}, bf16[256,768]{1,0:T(8,128)(2,1)}, u32[]{:S(2)}) copy-start(bf16[256,768]{1,0:T(8,128)(2,1)} %param.25) | copy-start | bytes 1179652
  244.1 73.4 %all-gather.6.cloned.1.call-start = ((), (), s32[]{:S(2)}) async-start(), calls=%async_computation.6 | async-start | bytes 1966080 | tf_op jit(solution)/shard_map/all_gather | solution.py:119
  281.3 64.6 %all-gather.8.cloned.1.call-start = ((), (), s32[]{:S(2)}) async-start(), calls=%async_computation.7 | async-start | bytes 1966080 | tf_op jit(solution)/shard_map/all_gather | solution.py:123
  317.5 6.3 %copy-start.1 = (bf16[256,3072]{1,0:T(8,128)(2,1)S(1)}, bf16[256,3072]{1,0:T(8,128)(2,1)}, u32[]{:S(2)}) copy-start(bf16[256,3072]{1,0:T(8,128)(2,1)} %all-gather.6.cloned.1.call-done) | copy-start | bytes 4718596
  320.3 32.0 %all-to-all-start = ((bf16[256,4,768]{2,0,1:T(8,128)(2,1)}), bf16[256,4,768]{2,0,1:T(8,128)(2,1)S(1)}, u32[]{:S(2)}, u32[]{:S(2)}) async-start(bf16[256,4,768]{2,0,1:T(8,128)(2,1)} %bitcast.49), calls=%async_computation.2 | async-start | bytes 3145728 | tf_op jit(solution)/shard_map/all_to_all | solution.py:124
  352.4 1.1 copy-start.2
Sparse Core Ops, SparseCore 0:
  9.6 108.6 all-gather.3
  130.4 76.7 reduce-scatter.2
  244.2 35.1 reduce-scatter.4
  281.5 36.0 all-gather.5
  319.0 26.8 all-gather.7

commit v2 on v1

--- a/solution.py
+++ b/solution.py
@@ -3,6 +3,8 @@
 import jax
 import jax.numpy as jnp
 from jax import lax
+from jax.experimental import pallas as pl
+from jax.experimental.pallas import tpu as pltpu
 from jax.sharding import PartitionSpec as P
 
 TD = 8192
@@ -64,6 +66,324 @@
     return jnp.transpose(attended, (2, 0, 1, 3)).reshape(row_count, key_heads * per_key * HEAD)
 
 
+CHUNKS = 8
+MESH = pl.DeviceIdType.MESH
+
+
+def project_kernel(
+    q_ref, k_ref, v_ref, res_ref, own_ref, out_ref,
+    kv, weights, attended, peak, total, mixed, sends, lands, far_lands,
+    kv_send, kv_recv, x_send, x_recv, s_send, s_recv, y_send, y_recv, f_send, f_recv,
+    z_send, z_recv, far_recv,
+):
+    group = lax.axis_index("groups")
+    c = lax.axis_index("ctx")
+    t = lax.axis_index("tp")
+    last = lax.axis_size("tp") - 1
+    x, core = c // 2, c % 2
+    sibling = {"ctx": 2 * x + 1 - core}
+    across = {"ctx": 2 * (1 - x) + core}
+    twin = {"groups": 1 - group}
+    dests = (c, 2 * x + 1 - core, 2 * (1 - x) + core, 2 * (1 - x) + 1 - core)
+    rows = q_ref.shape[0]
+    depth, width = own_ref.shape
+    cut = width // CHUNKS
+    half = depth // 2
+    groups_of = q_ref.shape[1] // k_ref.shape[1]
+    key_heads = k_ref.shape[1] // HEAD
+
+    barrier = pltpu.get_barrier_semaphore()
+    for peer in (sibling, across, twin):
+        pl.semaphore_signal(barrier, inc=1, device_id=peer, device_id_type=MESH)
+
+    @pl.when(t > 0)
+    def _():
+        pl.semaphore_signal(barrier, inc=1, device_id={"tp": t - 1}, device_id_type=MESH)
+
+    @pl.when(t < last)
+    def _():
+        pl.semaphore_signal(barrier, inc=1, device_id={"tp": t + 1}, device_id_type=MESH)
+
+    pl.semaphore_wait(barrier, 3 + (t > 0).astype(jnp.int32) + (t < last).astype(jnp.int32))
+
+    def remote(src, dst, send_sem, recv_sem, peer):
+        return pltpu.make_async_remote_copy(
+            src_ref=src, dst_ref=dst, send_sem=send_sem, recv_sem=recv_sem,
+            device_id=peer, device_id_type=MESH,
+        )
+
+    def kv_copy(slot, part, src, peer):
+        return remote(src, kv.at[slot, part], kv_send.at[slot, part], kv_recv.at[slot, part], peer)
+
+    def columns(j):
+        return pl.ds(pl.multiple_of(j * cut, cut), cut)
+
+    def half_rows(which):
+        return pl.ds(pl.multiple_of(which * half, half), half)
+
+    def across_copy(j):
+        where = (half_rows(group), columns(j))
+        return remote(
+            own_ref.at[where], weights.at[(1,) + where], x_send.at[j], x_recv.at[j], across
+        )
+
+    def sibling_copy(j):
+        where = (slice(None), columns(j))
+        return remote(
+            own_ref.at[where], weights.at[(0,) + where], s_send.at[j], s_recv.at[j], sibling
+        )
+
+    def twin_copy(j, which):
+        where = (1, half_rows(which), columns(j))
+        return remote(weights.at[where], weights.at[where], y_send.at[j], y_recv.at[j], twin)
+
+    def forward_copy(j, order, which):
+        where = (half_rows(which), columns(j))
+        return remote(
+            weights.at[(1,) + where], weights.at[(2,) + where],
+            f_send.at[order, j], f_recv.at[order, j], sibling,
+        )
+
+    own_kv = (k_ref, v_ref)
+
+    @pl.when(x == 0)
+    def _():
+        for part in range(2):
+            kv_copy(1, part, own_kv[part], across).start()
+
+    @pl.when(core == 0)
+    def _():
+        for part in range(2):
+            kv_copy(0, part, own_kv[part], sibling).start()
+
+    for j in range(2):
+        across_copy(j).start()
+        sibling_copy(j).start()
+
+    def block_scores(head, keys):
+        stacked = jnp.concatenate(
+            [
+                q_ref[:, (head * groups_of + g) * HEAD:(head * groups_of + g + 1) * HEAD]
+                for g in range(groups_of)
+            ],
+            axis=0,
+        )
+        return lax.dot_general(
+            stacked, keys, (((1,), (1,)), ((), ())), preferred_element_type=jnp.float32
+        ) * (1.0 / math.sqrt(HEAD))
+
+    for head in range(key_heads):
+        lanes = slice(head * HEAD, (head + 1) * HEAD)
+        scores = block_scores(head, k_ref[:, lanes])
+        query_row = lax.broadcasted_iota(jnp.int32, scores.shape, 0) % rows
+        key_row = lax.broadcasted_iota(jnp.int32, scores.shape, 1)
+        scores = jnp.where(key_row <= query_row, scores, -1e30)
+        top = jnp.max(scores, axis=1, keepdims=True)
+        exponent = jnp.exp(scores - top)
+        peak[head] = top
+        total[head] = jnp.sum(exponent, axis=1, keepdims=True)
+        mixed[head] = jnp.dot(
+            exponent.astype(jnp.bfloat16), v_ref[:, lanes], preferred_element_type=jnp.float32
+        )
+
+    def add_block(slot):
+        for head in range(key_heads):
+            lanes = slice(head * HEAD, (head + 1) * HEAD)
+            scores = block_scores(head, kv[slot, 0, :, lanes])
+            top = jnp.maximum(peak[head], jnp.max(scores, axis=1, keepdims=True))
+            shrink = jnp.exp(peak[head] - top)
+            exponent = jnp.exp(scores - top)
+            peak[head] = top
+            total[head] = total[head] * shrink + jnp.sum(exponent, axis=1, keepdims=True)
+            mixed[head] = mixed[head] * shrink + jnp.dot(
+                exponent.astype(jnp.bfloat16), kv[slot, 1, :, lanes],
+                preferred_element_type=jnp.float32,
+            )
+
+    @pl.when(core == 1)
+    def _():
+        for part in range(2):
+            kv_copy(0, part, own_kv[part], sibling).wait_recv()
+        add_block(0)
+
+    @pl.when(x == 1)
+    def _():
+        for part in range(2):
+            kv_copy(1, part, own_kv[part], across).wait_recv()
+        for part in range(2):
+            kv_copy(2, part, kv.at[1, part], sibling).start()
+        add_block(1)
+        for part in range(2):
+            kv_copy(2, part, kv.at[1, part], sibling).wait_recv()
+        add_block(2)
+
+    for j in range(2, CHUNKS):
+        across_copy(j).start()
+        sibling_copy(j).start()
+
+    for head in range(key_heads):
+        result = (mixed[head] / total[head]).astype(jnp.bfloat16)
+        for g in range(groups_of):
+            at = (head * groups_of + g) * HEAD
+            attended[:, at:at + HEAD] = result[g * rows:(g + 1) * rows]
+
+    def z_copy(i, j, peer):
+        return remote(
+            sends.at[i, j], lands.at[i, j], z_send.at[i, j], z_recv.at[i, j], {"tp": peer}
+        )
+
+    def far_copy(i, j, peer):
+        return remote(
+            sends.at[i, j], far_lands.at[j], z_send.at[i, j], far_recv.at[j], {"tp": peer}
+        )
+
+    def process(i, j, block):
+        dest = dests[i]
+        product = jnp.dot(attended[...], block, preferred_element_type=jnp.float32)
+        towards = jnp.where(dest > t, t + 1, t - 1)
+        incoming = ((dest > t) & (t > 0)) | ((dest < t) & (t < last))
+
+        @pl.when(dest == t)
+        def _():
+            out_ref[:, columns(j)] = product + res_ref[:, columns(j)].astype(jnp.float32)
+
+        @pl.when((dest != t) & incoming)
+        def _():
+            z_copy(i, j, towards).wait_recv()
+            sends[i, j] = (product + lands[i, j].astype(jnp.float32)).astype(jnp.bfloat16)
+
+        @pl.when((dest != t) & jnp.logical_not(incoming))
+        def _():
+            sends[i, j] = product.astype(jnp.bfloat16)
+
+        @pl.when((dest != t) & (dest != t - 1))
+        def _():
+            z_copy(i, j, towards).start()
+
+        @pl.when(dest == t - 1)
+        def _():
+            far_copy(i, j, towards).start()
+
+    def step(j, carry):
+        @pl.when(j < CHUNKS)
+        def _():
+            process(0, j, own_ref[:, columns(j)])
+            sibling_copy(j).wait_recv()
+            process(1, j, weights[0, :, columns(j)])
+            across_copy(j).wait_recv()
+            twin_copy(j, group).start()
+            forward_copy(j, 0, group).start()
+
+        @pl.when(j > 0)
+        def _():
+            p = j - 1
+            twin_copy(p, 1 - group).wait_recv()
+            forward_copy(p, 1, 1 - group).start()
+            process(2, p, weights[1, :, columns(p)])
+            forward_copy(p, 0, group).wait_recv()
+            forward_copy(p, 1, 1 - group).wait_recv()
+            process(3, p, weights[2, :, columns(p)])
+
+        return carry
+
+    lax.fori_loop(0, CHUNKS + 1, step, 0)
+
+    def finish(j, carry):
+        for i in range(4):
+            @pl.when((dests[i] == t) & (t > 0))
+            def _():
+                z_copy(i, j, t).wait_recv()
+                out_ref[:, columns(j)] += lands[i, j].astype(jnp.float32)
+
+        @pl.when(t < last)
+        def _():
+            far_copy(0, j, t).wait_recv()
+            out_ref[:, columns(j)] += far_lands[j].astype(jnp.float32)
+
+        return carry
+
+    lax.fori_loop(0, CHUNKS, finish, 0)
+
+    def drain(j, carry):
+        across_copy(j).wait_send()
+        sibling_copy(j).wait_send()
+        twin_copy(j, group).wait_send()
+        forward_copy(j, 0, group).wait_send()
+        forward_copy(j, 1, 1 - group).wait_send()
+        for i in range(4):
+            @pl.when(dests[i] != t)
+            def _():
+                z_copy(i, j, t).wait_send()
+        return carry
+
+    lax.fori_loop(0, CHUNKS, drain, 0)
+
+    @pl.when(x == 0)
+    def _():
+        for part in range(2):
+            kv_copy(1, part, own_kv[part], across).wait_send()
+
+    @pl.when(core == 0)
+    def _():
+        for part in range(2):
+            kv_copy(0, part, own_kv[part], sibling).wait_send()
+
+    @pl.when(x == 1)
+    def _():
+        for part in range(2):
+            kv_copy(2, part, kv.at[1, part], sibling).wait_send()
+
+
+def hidden_fused(queries, keys, values, teacher_residual, teacher_out):
+    rows, key_width = keys.shape
+    depth, width = teacher_out.shape
+    cut = width // CHUNKS
+    key_heads = key_width // HEAD
+    stacked = rows * queries.shape[1] // key_width
+    dma = pltpu.SemaphoreType.DMA
+    vmem = pl.BlockSpec(memory_space=pltpu.VMEM)
+    return pl.pallas_call(
+        project_kernel,
+        out_shape=jax.ShapeDtypeStruct((rows, width), jnp.float32),
+        in_specs=[vmem] * 5,
+        out_specs=vmem,
+        scratch_shapes=[
+            pltpu.VMEM((3, 2, rows, key_width), jnp.bfloat16),
+            pltpu.VMEM((3, depth, width), jnp.bfloat16),
+            pltpu.VMEM((rows, depth), jnp.bfloat16),
+            pltpu.VMEM((key_heads, stacked, 1), jnp.float32),
+            pltpu.VMEM((key_heads, stacked, 1), jnp.float32),
+            pltpu.VMEM((key_heads, stacked, HEAD), jnp.float32),
+            pltpu.VMEM((4, CHUNKS, rows, cut), jnp.bfloat16),
+            pltpu.VMEM((4, CHUNKS, rows, cut), jnp.bfloat16),
+            pltpu.VMEM((CHUNKS, rows, cut), jnp.bfloat16),
+            dma((3, 2)), dma((3, 2)),
+            dma((CHUNKS,)), dma((CHUNKS,)),
+            dma((CHUNKS,)), dma((CHUNKS,)),
+            dma((CHUNKS,)), dma((CHUNKS,)),
+            dma((2, CHUNKS)), dma((2, CHUNKS)),
+            dma((4, CHUNKS)), dma((4, CHUNKS)),
+            dma((CHUNKS,)),
+        ],
+        compiler_params=pltpu.CompilerParams(
+            collective_id=0, has_side_effects=True, vmem_limit_bytes=48 * 1024 * 1024
+        ),
+    )(queries, keys, values, teacher_residual, teacher_out)
+
+
+def hidden_plain(queries, keys, values, teacher_residual, teacher_out):
+    attended = attend_local(queries, keys, values)
+    column_terms = jnp.dot(
+        attended,
+        lax.all_gather(teacher_out, "ctx", axis=1, tiled=True),
+        preferred_element_type=jnp.float32,
+    )
+    summed = lax.psum_scatter(
+        column_terms.astype(jnp.bfloat16), "tp", scatter_dimension=1, tiled=True
+    ).astype(jnp.float32)
+    return teacher_residual.astype(jnp.float32) + summed
+
+
 def body(
     queries,
     keys,
@@ -79,18 +399,10 @@
     student_out,
     student_residual,
 ):
-    attended = attend_local(queries, keys, values)
-    row_count = attended.shape[0]
-    feature_width = teacher_residual.shape[1]
-    column_terms = jnp.dot(
-        attended,
-        lax.all_gather(teacher_out, "ctx", axis=1, tiled=True),
-        preferred_element_type=jnp.float32,
-    )
-    summed = lax.psum_scatter(
-        column_terms.astype(jnp.bfloat16), "tp", scatter_dimension=1, tiled=True
-    ).astype(jnp.float32)
-    hidden = teacher_residual.astype(jnp.float32) + summed
+    sizes = (lax.axis_size("groups"), lax.axis_size("ctx"), lax.axis_size("tp"))
+    hidden_of = hidden_fused if sizes == (2, 4, 4) else hidden_plain
+    hidden = hidden_of(queries, keys, values, teacher_residual, teacher_out)
+    row_count, feature_width = teacher_residual.shape
     squares = lax.psum(jnp.sum(hidden * hidden, axis=1), "tp")
     gain_share = lax.dynamic_slice_in_dim(
         teacher_gain, lax.axis_index("tp") * feature_width, feature_width, 0

time: 366 us -> 302 us (0.83)
  waiting for transfers between devices: 262 us -> 113 us
  Pallas kernels: 0 us -> 106 us
  matrix products: 40.2 us -> 24.4 us
  other arithmetic: 7.15 us -> 2.36 us
    pallas_call x0 -> x1, Pallas kernels: none -> 106 us  [hidden_fused(): pl.pallas_call(project_kernel, out_shape=jax.ShapeDtypeStruct((rows, widt...]
    all_gather x1 -> x0, waiting for transfers between devices: 87.7 us -> none  [body(): lax.all_gather(teacher_out, 'ctx', axis=1, tiled=True)]
    reduce_scatter x1 -> x0, waiting for transfers between devices: 76.1 us -> none  [body(): lax.psum_scatter(column_terms.astype(jnp.bfloat16), 'tp', scatter_dimensi...]
    all_gather x2 -> x0, blocking collectives: 15.9 us -> none  [the longest x1 8.62 us: attend_local(): value_piece = lax.all_gather(values, 'ctx', axis=0, tiled=True)]
    dot_general x3 -> x0, matrix products: 15.8 us -> none  [the longest x1 12 us: body(): jnp.dot(attended, lax.all_gather(teacher_out, 'ctx', axis=1, tiled=True),...]
    ppermute x1, waiting for transfers between devices: 3.57 us -> 17.4 us  [padded(): lax.ppermute(head, axis, [((i + 1) % count, i) for i in range(ends)])]
    psum x1, blocking collectives: 10.9 us -> 23.7 us  [body(): squares = lax.psum(jnp.sum(hidden * hidden, axis=1), 'tp')]
    unnamed x22 -> x21, local copies, waits for them, and re-layouts: 3.42 us -> 7.18 us
  transfers between devices with their start and end apart: 8 -> 6, of which waited for: 7 -> 5; matrix products, arithmetic and copies ran while one was open for 4% -> 3% of each run, Pallas kernels for 0% -> 0%
where the time goes in v2:
time: 302 us
  waiting for transfers between devices  113 us (37%)
  Pallas kernels  106 us (35%)
  matrix products  24.4 us (8%)
  blocking collectives  23.7 us (8%)
  between operations  14.6 us (5%)
  local copies, waits for them, and re-layouts  10.5 us (3%)
  starting transfers between devices  6.58 us (2%)
    pallas_call x1, Pallas kernels, hidden_fused(): pl.pallas_call(project_kernel, out_shape=jax.ShapeDtypeStruct((rows, widt...  106 us
    reduce_scatter x1, waiting for transfers between devices, body(): lax.psum_scatter((student_term - target_term).astype(jnp.bfloat16), 'tp',...  36.1 us
    all_gather x1, waiting for transfers between devices, body(): grad_full = lax.all_gather(grad_hidden, 'tp', axis=1, tiled=True)  35.6 us
    psum x1, blocking collectives, body(): squares = lax.psum(jnp.sum(hidden * hidden, axis=1), 'tp')  23.7 us
    ppermute x1, waiting for transfers between devices, padded(): lax.ppermute(head, axis, [((i + 1) % count, i) for i in range(ends)])  17.4 us
    all_gather x1, waiting for transfers between devices, body(): context_rows = lax.all_gather(student_context, 'ctx', axis=0, tiled=True)  17.2 us
    dot_general x1, matrix products, body(): target_term = jnp.dot(pooled, projector, preferred_element_type=jnp.float32)  10.2 us
    unnamed x21, local copies, waits for them, and re-layouts  7.18 us
  transfers between devices with their start and end apart: 6, of which 5 were waited for; matrix products, arithmetic and copies ran while one was open for 3% of the time, Pallas kernels for 0%

profile of v2, /device:TPU:0, one launch (start us, length us, event | category | flops | bytes accessed | tf_op | source)
XLA Modules:
  0.0 301.7 jit_solution(2342502415002367090)
XLA Ops:
  7.2 1.2 copy-done
  8.4 1.0 copy-done.1
  9.5 0.9 copy-done.2
  10.4 0.9 copy-done.3
  11.3 106.3 %shard_map.140 = f32[256,2048]{1,0:T(8,128)S(1)} custom-call(bf16[256,1024]{1,0:T(8,128)(2,1)S(1)} %copy-done.1, bf16[256,256]{1,0:T(8,128)(2,1)S(1)} %copy-done.2, bf16[256,256]{1,0:T(8,128)(2,1)S(1)} %copy-done.3, bf16[256,2048]{1,0:T(8,128)(2,1)S(1)} %copy-done, bf16[1024,2048]{1,0:T(8,128)(2,1)} %own_ref.1), custom_call_target="tpu_custom_call" | custom-call | tf_op jit(solution)/shard_map/pallas_call | solution.py:345
  117.8 23.7 %psum.7 = f32[256]{0:T(256)S(1)} all-reduce(f32[256]{0:T(256)S(1)} %multiply_reduce_fusion), channel_id=1, replica_groups=mesh['groups'=2,'ctx'=4,'tp'=4] {'tp'}, use_global_device_ids=true, to_apply=%region_1.0 | all-reduce | flops 256 | bytes 2048 | tf_op jit(solution)/shard_map/psum | solution.py:406
  141.5 0.7 dynamic_slice.3
  142.5 1.3 collective-permute-start
  143.8 1.5 collective-permute-start.1
  145.3 17.4 %collective-permute-done.1 = bf16[16,2048]{1,0:T(8,128)(2,1)S(1)} collective-permute-done((bf16[16,2048]{1,0:T(8,128)(2,1)S(1)}, bf16[16,2048]{1,0:T(8,128)(2,1)S(1)}, u32[]{:S(2)}, u32[]{:S(2)}) %collective-permute-start.1) | collective-permute-done | bytes 65568 | tf_op jit(solution)/shard_map/ppermute | solution.py:27
  162.7 10.2 %fusion.2 = f32[256,3072]{1,0:T(8,128)} fusion(bf16[2048,3072]{1,0:T(8,128)(2,1)} %param.19, bf16[16,2048]{1,0:T(8,128)(2,1)S(1)} %collective-permute-done.1, bf16[256,2048]{1,0:T(8,128)(2,1)S(1)} %multiply_convert_fusion, bf16[16,2048]{1,0:T(8,128)(2,1)S(1)} %collective-permute-done, f32[256]{0:T(256)S(1)} %subtract_convert_fusion, ...), kind=kOutput, calls=%fused_computation.9 | convolution fusion | flops 3528024064 | bytes 16912512 | tf_op jit(solution)/shard_map/dot_general | solution.py:422
  172.9 6.0 %fusion = bf16[256,3072]{1,0:T(8,128)(2,1)} fusion(f32[256,3072]{1,0:T(8,128)} %fusion.2, bf16[256,768]{1,0:T(8,128)(2,1)S(1)} %copy-done.6, bf16[768,3072]{1,0:T(8,128)(2,1)} %param.24), kind=kOutput, calls=%fused_computation.1 | convolution fusion | flops 1209532416 | bytes 9830400 | tf_op jit(solution)/shard_map/dot_general | solution.py:421
  179.6 36.1 %reduce-scatter.2.cloned.1.call-done = bf16[256,768]{1,0:T(8,128)(2,1)} async-done(((bf16[256,3072]{1,0:T(8,128)(2,1)}), bf16[256,768]{1,0:T(8,128)(2,1)}) %reduce-scatter.2.cloned.1.call-update) | async-done | bytes 393232 | tf_op jit(solution)/shard_map/reduce_scatter | solution.py:423
  215.7 1.9 select_convert_fusion
  217.6 0.7 all-gather.5.cloned.1.call-update
  218.3 35.6 %all-gather.3.cloned.1.call-done = bf16[256,3072]{1,0:T(8,128)(2,1)} async-done(((bf16[256,768]{1,0:T(8,128)(2,1)}), bf16[256,3072]{1,0:T(8,128)(2,1)}) %all-gather.3.cloned.1.call-update) | async-done | bytes 1572880 | tf_op jit(solution)/shard_map/all_gather | solution.py:431
  253.9 2.7 copy.20
  256.6 3.7 %all-to-all-start = ((bf16[256,4,768]{2,0,1:T(8,128)(2,1)}), bf16[256,4,768]{2,0,1:T(8,128)(2,1)S(1)}, u32[]{:S(2)}, u32[]{:S(2)}) async-start(bf16[256,4,768]{2,0,1:T(8,128)(2,1)} %bitcast.16), calls=%async_computation.1 | async-start | bytes 3145728 | tf_op jit(solution)/shard_map/all_to_all | solution.py:436
  260.3 4.9 %convolution_convert_fusion = bf16[256,768]{1,0:T(8,128)(2,1)} fusion(bf16[256,3072]{1,0:T(8,128)(2,1)S(1)} %copy-done.4, bf16[768,3072]{1,0:T(8,128)(2,1)} %param.24), kind=kOutput, calls=%fused_computation.8 | convolution fusion | flops 1208156160 | bytes 6684672 | tf_op jit(solution)/shard_map/dot_general | solution.py:432
  265.2 17.2 %all-gather.5.cloned.1.call-done = bf16[1024,768]{1,0:T(8,128)(2,1)} async-done(((bf16[256,768]{1,0:T(8,128)(2,1)}), bf16[1024,768]{1,0:T(8,128)(2,1)}) %all-gather.5.cloned.1.call-update) | async-done | bytes 1572880 | tf_op jit(solution)/shard_map/all_gather | solution.py:435
  282.4 6.4 %all-to-all-done = bf16[256,4,768]{2,0,1:T(8,128)(2,1)S(1)} async-done(((bf16[256,4,768]{2,0,1:T(8,128)(2,1)}), bf16[256,4,768]{2,0,1:T(8,128)(2,1)S(1)}, u32[]{:S(2)}, u32[]{:S(2)}) %all-to-all-start) | async-done | bytes 1572896 | tf_op jit(solution)/shard_map/all_to_all | solution.py:436
  288.8 1.1 copy-done.5
  289.9 3.3 %convolution_bitcast_fusion = f32[768,768]{0,1:T(8,128)S(1)} fusion(bf16[1024,768]{1,0:T(8,128)(2,1)} %bitcast.19, bf16[1024,768]{1,0:T(8,128)(2,1)} %all-gather.5.cloned.1.call-done), kind=kOutput, calls=%fused_computation.6 | convolution fusion | flops 1207959552 | bytes 5505024 | tf_op jit(solution)/shard_map/dot_general | solution.py:437
  293.2 2.0 copy.17
  (28 shorter events, 0.7 us)
Async XLA Ops:
  7.2 208.5 %reduce-scatter.2.cloned.1.call-start = ((), (), s32[]{:S(2)}) async-start(), calls=%async_computation.2 | async-start | bytes 1966080 | tf_op jit(solution)/shard_map/reduce_scatter | solution.py:423
  7.2 1.2 copy-start
  8.4 1.0 copy-start.1
  9.5 0.9 copy-start.2
  10.4 0.9 copy-start.3
  117.8 27.5 %copy-start.8 = (s32[256]{0:T(256)S(1)}, s32[256]{0:T(256)}, u32[]{:S(2)}) copy-start(s32[256]{0:T(256)} %param.21) | copy-start | bytes 3076
  117.8 27.5 %copy-start.9 = (s32[256]{0:T(256)S(1)}, s32[256]{0:T(256)}, u32[]{:S(2)}) copy-start(s32[256]{0:T(256)} %param.20) | copy-start | bytes 3076
  142.5 2.8 collective-permute-start
  143.8 18.9 %collective-permute-start.1 = (bf16[16,2048]{1,0:T(8,128)(2,1)S(1)}, bf16[16,2048]{1,0:T(8,128)(2,1)S(1)}, u32[]{:S(2)}, u32[]{:S(2)}) collective-permute-start(bf16[16,2048]{1,0:T(8,128)(2,1)S(1)} %get-tuple-element.7), channel_id=1, source_target_pairs={{4,0},{8,4},{12,8},{5,1},{9,5},{13,9},{6,2},{10,6},{14,10},{7,3},{... | collective-permute-start | bytes 196616 | tf_op jit(solution)/shard_map/ppermute | solution.py:27
  145.3 27.6 %copy-start.6 = (bf16[256,768]{1,0:T(8,128)(2,1)S(1)}, bf16[256,768]{1,0:T(8,128)(2,1)}, u32[]{:S(2)}) copy-start(bf16[256,768]{1,0:T(8,128)(2,1)} %param.23) | copy-start | bytes 1179652
  172.9 42.8 %copy-start.7 = (bf16[256,768]{1,0:T(8,128)(2,1)S(1)}, bf16[256,768]{1,0:T(8,128)(2,1)}, u32[]{:S(2)}) copy-start(bf16[256,768]{1,0:T(8,128)(2,1)} %param.25) | copy-start | bytes 1179652
  178.9 75.0 %all-gather.3.cloned.1.call-start = ((), (), s32[]{:S(2)}) async-start(), calls=%async_computation.3 | async-start | bytes 1966080 | tf_op jit(solution)/shard_map/all_gather | solution.py:431
  217.6 64.8 %all-gather.5.cloned.1.call-start = ((), (), s32[]{:S(2)}) async-start(), calls=%async_computation.4 | async-start | bytes 1966080 | tf_op jit(solution)/shard_map/all_gather | solution.py:435
  256.6 3.7 %copy-start.4 = (bf16[256,3072]{1,0:T(8,128)(2,1)S(1)}, bf16[256,3072]{1,0:T(8,128)(2,1)}, u32[]{:S(2)}) copy-start(bf16[256,3072]{1,0:T(8,128)(2,1)} %all-gather.3.cloned.1.call-done) | copy-start | bytes 4718596
  256.6 32.2 %all-to-all-start = ((bf16[256,4,768]{2,0,1:T(8,128)(2,1)}), bf16[256,4,768]{2,0,1:T(8,128)(2,1)S(1)}, u32[]{:S(2)}, u32[]{:S(2)}) async-start(bf16[256,4,768]{2,0,1:T(8,128)(2,1)} %bitcast.16), calls=%async_computation.1 | async-start | bytes 3145728 | tf_op jit(solution)/shard_map/all_to_all | solution.py:436
  288.8 1.1 copy-start.5
Sparse Core Ops, SparseCore 0:
  179.0 36.5 reduce-scatter.1
  217.8 36.0 all-gather.2
  255.5 26.8 all-gather.4

commit v3 on v2

--- a/solution.py
+++ b/solution.py
@@ -384,6 +384,258 @@
     return teacher_residual.astype(jnp.float32) + summed
 
 
+HALVES = 2
+
+
+def gradient_kernel(
+    pooled_ref, proj_ref, sc_ref, so_ref, res_ref, valid_ref, gout_ref, gctx_ref,
+    sends, lands, far_lands, gap, grads, crossed, contexts, context_sum,
+    z_send, z_recv, far_recv, r_send, r_recv, l_send, l_recv, e_send, e_recv, c_send, c_recv,
+):
+    c = lax.axis_index("ctx")
+    t = lax.axis_index("tp")
+    ranks = lax.axis_size("tp")
+    last = ranks - 1
+    shards = lax.axis_size("ctx")
+    block = res_ref.shape[1]
+    cut = block // HALVES
+
+    barrier = pltpu.get_barrier_semaphore()
+    for peer in range(shards):
+        @pl.when(c != peer)
+        def _():
+            pl.semaphore_signal(barrier, inc=1, device_id={"ctx": peer}, device_id_type=MESH)
+
+    @pl.when(t > 0)
+    def _():
+        pl.semaphore_signal(barrier, inc=1, device_id={"tp": t - 1}, device_id_type=MESH)
+
+    @pl.when(t < last)
+    def _():
+        pl.semaphore_signal(barrier, inc=1, device_id={"tp": t + 1}, device_id_type=MESH)
+
+    pl.semaphore_wait(
+        barrier, shards - 1 + (t > 0).astype(jnp.int32) + (t < last).astype(jnp.int32)
+    )
+
+    def remote(src, dst, send_sem, recv_sem, peer):
+        return pltpu.make_async_remote_copy(
+            src_ref=src, dst_ref=dst, send_sem=send_sem, recv_sem=recv_sem,
+            device_id=peer, device_id_type=MESH,
+        )
+
+    def context_copy(sender, peer):
+        return remote(
+            sc_ref, contexts.at[sender], c_send.at[peer], c_recv.at[sender], {"ctx": peer}
+        )
+
+    def z_copy(d, h, peer):
+        return remote(
+            sends.at[d, h], lands.at[d, h], z_send.at[d, h], z_recv.at[d, h], {"tp": peer}
+        )
+
+    def far_copy(d, h, peer):
+        return remote(
+            sends.at[d, h], far_lands.at[h], z_send.at[d, h], far_recv.at[h], {"tp": peer}
+        )
+
+    def right_copy(s, h):
+        return remote(
+            grads.at[s, h], grads.at[s, h], r_send.at[s, h], r_recv.at[s, h],
+            {"tp": jnp.minimum(t + 1, last)},
+        )
+
+    def left_copy(s, h):
+        return remote(
+            grads.at[s, h], grads.at[s, h], l_send.at[s, h], l_recv.at[s, h],
+            {"tp": jnp.maximum(t - 1, 0)},
+        )
+
+    def cross_copy(s, h, sender):
+        return remote(
+            grads.at[s, h], crossed.at[sender, h], e_send.at[s, h], e_recv.at[sender, h],
+            {"ctx": s},
+        )
+
+    for h in range(HALVES):
+        for d in (3, 0, 2, 1):
+            lanes = slice(d * block + h * cut, d * block + (h + 1) * cut)
+            product = jnp.dot(
+                sc_ref[...], so_ref[:, lanes], preferred_element_type=jnp.float32
+            ) - jnp.dot(pooled_ref[...], proj_ref[:, lanes], preferred_element_type=jnp.float32)
+            towards = jnp.where(t < d, t + 1, t - 1)
+            incoming = ((t < d) & (t > 0)) | ((t > d) & (t < last))
+
+            @pl.when(t == d)
+            def _():
+                gap[h] = product
+
+            @pl.when((t != d) & incoming)
+            def _():
+                z_copy(d, h, towards).wait_recv()
+                sends[d, h] = (product + lands[d, h].astype(jnp.float32)).astype(jnp.bfloat16)
+
+            @pl.when((t != d) & jnp.logical_not(incoming))
+            def _():
+                sends[d, h] = product.astype(jnp.bfloat16)
+
+            @pl.when((t != d) & (t != d + 1))
+            def _():
+                z_copy(d, h, towards).start()
+
+            @pl.when(t == d + 1)
+            def _():
+                far_copy(d, h, towards).start()
+
+    for peer in range(shards):
+        @pl.when(c != peer)
+        def _():
+            context_copy(c, peer).start()
+
+    for h in range(HALVES):
+        @pl.when(t > 0)
+        def _():
+            z_copy(t, h, t).wait_recv()
+            gap[h] += lands[t, h].astype(jnp.float32)
+
+        @pl.when(t < last)
+        def _():
+            far_copy(t, h, t).wait_recv()
+            gap[h] += far_lands[h].astype(jnp.float32)
+
+        student = res_ref[:, h * cut:(h + 1) * cut].astype(jnp.float32) + gap[h]
+        grads[t, h] = jnp.where(valid_ref[...] > 0, student, 0.0).astype(jnp.bfloat16)
+
+        @pl.when(t < last)
+        def _():
+            right_copy(t, h).start()
+
+        @pl.when(t > 0)
+        def _():
+            left_copy(t, h).start()
+
+    def cross(s, h):
+        @pl.when(s != c)
+        def _():
+            cross_copy(s, h, c).start()
+
+    def accumulate(s, h):
+        lanes = pl.ds(pl.multiple_of(s * block + h * cut, cut), cut)
+        context_sum[...] += lax.dot_general(
+            grads[s, h], so_ref[:, lanes], (((1,), (1,)), ((), ())),
+            preferred_element_type=jnp.float32,
+        )
+
+    context_sum[...] = jnp.zeros_like(context_sum)
+    for h in range(HALVES):
+        cross(t, h)
+    for h in range(HALVES):
+        accumulate(t, h)
+    for hop in range(1, 4):
+        for h in range(HALVES):
+            @pl.when(t >= hop)
+            def _():
+                right_copy(t - hop, h).wait_recv()
+
+                @pl.when(t < last)
+                def _():
+                    right_copy(t - hop, h).start()
+
+                cross(t - hop, h)
+
+            @pl.when(t + hop <= last)
+            def _():
+                left_copy(t + hop, h).wait_recv()
+
+                @pl.when(t > 0)
+                def _():
+                    left_copy(t + hop, h).start()
+
+                cross(t + hop, h)
+
+            @pl.when(t >= hop)
+            def _():
+                accumulate(t - hop, h)
+
+            @pl.when(t + hop <= last)
+            def _():
+                accumulate(t + hop, h)
+
+    gctx_ref[...] = context_sum[...].astype(jnp.bfloat16)
+
+    def outer(context, grad):
+        return lax.dot_general(
+            context, grad, (((0,), (0,)), ((), ())), preferred_element_type=jnp.float32
+        )
+
+    for h in range(HALVES):
+        gout_ref[:, h * cut:(h + 1) * cut] = outer(sc_ref[...], grads[c, h])
+    for sender in range(shards):
+        @pl.when(c != sender)
+        def _():
+            context_copy(sender, c).wait_recv()
+            for h in range(HALVES):
+                cross_copy(c, h, sender).wait_recv()
+                gout_ref[:, h * cut:(h + 1) * cut] += outer(contexts[sender], crossed[sender, h])
+
+    for s in range(ranks):
+        @pl.when(c != s)
+        def _():
+            context_copy(c, s).wait_send()
+
+        for h in range(HALVES):
+            @pl.when(t != s)
+            def _():
+                z_copy(s, h, t).wait_send()
+
+            @pl.when(c != s)
+            def _():
+                cross_copy(s, h, c).wait_send()
+
+            @pl.when((t >= s) & (t < last))
+            def _():
+                right_copy(s, h).wait_send()
+
+            @pl.when((t <= s) & (t > 0))
+            def _():
+                left_copy(s, h).wait_send()
+
+
+def gradients_fused(pooled, projector, student_context, student_out, student_residual, valid_rows):
+    rows, block = student_residual.shape
+    cut = block // HALVES
+    dma = pltpu.SemaphoreType.DMA
+    vmem = pl.BlockSpec(memory_space=pltpu.VMEM)
+    pieces = pltpu.VMEM((4, HALVES, rows, cut), jnp.bfloat16)
+    pair = dma((4, HALVES))
+    return pl.pallas_call(
+        gradient_kernel,
+        out_shape=(
+            jax.ShapeDtypeStruct((block, block), jnp.float32),
+            jax.ShapeDtypeStruct((rows, block), jnp.bfloat16),
+        ),
+        in_specs=[vmem] * 6,
+        out_specs=(vmem, vmem),
+        scratch_shapes=[
+            pieces,
+            pieces,
+            pltpu.VMEM((HALVES, rows, cut), jnp.bfloat16),
+            pltpu.VMEM((HALVES, rows, cut), jnp.float32),
+            pieces,
+            pieces,
+            pltpu.VMEM((4, rows, block), jnp.bfloat16),
+            pltpu.VMEM((rows, block), jnp.float32),
+            pair, pair, dma((HALVES,)), pair, pair, pair, pair, pair, pair, dma((4,)), dma((4,)),
+        ],
+        compiler_params=pltpu.CompilerParams(
+            collective_id=1, has_side_effects=True, vmem_limit_bytes=48 * 1024 * 1024
+        ),
+    )(
+        pooled, projector, student_context, student_out, student_residual,
+        valid_rows.astype(jnp.float32)[:, None],
+    )
+
+
 def body(
     queries,
     keys,
@@ -418,13 +670,16 @@
     span_sums = jnp.dot(inside.astype(jnp.bfloat16), extended, preferred_element_type=jnp.float32)
     lengths = (span_ends - span_starts).astype(jnp.float32)
     pooled = (span_sums / lengths[:, None]).astype(jnp.bfloat16)
+    valid_rows = jnp.arange(row_count, dtype=jnp.int32) < aligned_counts[0]
+    if sizes == (2, 4, 4):
+        return gradients_fused(
+            pooled, projector, student_context, student_out, student_residual, valid_rows
+        )
     student_term = jnp.dot(student_context, student_out, preferred_element_type=jnp.float32)
     target_term = jnp.dot(pooled, projector, preferred_element_type=jnp.float32)
     residual_gap = lax.psum_scatter(
         (student_term - target_term).astype(jnp.bfloat16), "tp", scatter_dimension=1, tiled=True
     ).astype(jnp.float32)
-    local_rows = jnp.arange(row_count, dtype=jnp.int32)
-    valid_rows = local_rows < aligned_counts[0]
     grad_hidden = jnp.where(
         valid_rows[:, None], student_residual.astype(jnp.float32) + residual_gap, 0.0
     ).astype(jnp.bfloat16)

time: 302 us -> 243 us (0.80)
  waiting for transfers between devices: 113 us -> 16 us
  Pallas kernels: 106 us -> 190 us
  matrix products: 24.4 us -> 0.76 us
  between operations: 14.6 us -> 1.45 us
  starting transfers between devices: 6.58 us -> 2.59 us
  local copies, waits for them, and re-layouts: 10.5 us -> 6.96 us
    pallas_call x0 -> x1, Pallas kernels: none -> 83.2 us  [gradients_fused(): pl.pallas_call(gradient_kernel, out_shape=(jax.ShapeDtypeStruct((block, b...]
    all_gather x2 -> x0, waiting for transfers between devices: 52.8 us -> none  [the longest x1 35.6 us: body(): grad_full = lax.all_gather(grad_hidden, 'tp', axis=1, tiled=True)]
    reduce_scatter x1 -> x0, waiting for transfers between devices: 36.1 us -> none  [body(): lax.psum_scatter((student_term - target_term).astype(jnp.bfloat16), 'tp',...]
    dot_general x4 -> x1, matrix products: 24.4 us -> 0.76 us  [body(): jnp.dot(inside.astype(jnp.bfloat16), extended, preferred_element_type=jnp...]
    all_to_all x1 -> x0, waiting for transfers between devices: 6.4 us -> none  [body(): lax.all_to_all(grad_full, 'ctx', split_axis=1, concat_axis=0, tiled=True)]
    all_to_all x1 -> x0, starting transfers between devices: 3.69 us -> none  [body(): lax.all_to_all(grad_full, 'ctx', split_axis=1, concat_axis=0, tiled=True)]
    unnamed x21 -> x18, local copies, waits for them, and re-layouts: 7.18 us -> 6.24 us
  transfers between devices with their start and end apart: 6 -> 2, of which waited for: 5 -> 1; matrix products, arithmetic and copies ran while one was open for 3% -> 0% of each run, Pallas kernels for 0% -> 0%
where the time goes in v3:
time: 243 us; the launch traced here: 241 us
  Pallas kernels  190 us (78%)
  blocking collectives  23.7 us (10%)
  waiting for transfers between devices  16 us (7%)
  local copies, waits for them, and re-layouts  6.96 us (3%)
  starting transfers between devices  2.59 us (1%)
    pallas_call x1, Pallas kernels, hidden_fused(): pl.pallas_call(project_kernel, out_shape=jax.ShapeDtypeStruct((rows, widt...  106 us
    pallas_call x1, Pallas kernels, gradients_fused(): pl.pallas_call(gradient_kernel, out_shape=(jax.ShapeDtypeStruct((block, b...  83.2 us
    psum x1, blocking collectives, body(): squares = lax.psum(jnp.sum(hidden * hidden, axis=1), 'tp')  23.7 us
    ppermute x1, waiting for transfers between devices, padded(): lax.ppermute(head, axis, [((i + 1) % count, i) for i in range(ends)])  16 us
    unnamed x18, local copies, waits for them, and re-layouts  6.24 us
  transfers between devices with their start and end apart: 2, of which 1 were waited for; matrix products, arithmetic and copies ran while one was open for 0% of the time, Pallas kernels for 0%

profile of v3, /device:TPU:0, one launch (start us, length us, event | category | flops | bytes accessed | tf_op | source)
XLA Modules:
  0.0 241.5 jit_solution(7877178402949854859)
XLA Ops:
  0.6 0.0 copy-start
  0.6 1.2 copy-done
  1.9 1.0 copy-done.1
  2.9 0.9 copy-done.4
  3.8 0.9 copy-done.5
  4.7 106.3 %shard_map.140 = f32[256,2048]{1,0:T(8,128)S(1)} custom-call(bf16[256,1024]{1,0:T(8,128)(2,1)S(1)} %copy-done.1, bf16[256,256]{1,0:T(8,128)(2,1)S(1)} %copy-done.4, bf16[256,256]{1,0:T(8,128)(2,1)S(1)} %copy-done.5, bf16[256,2048]{1,0:T(8,128)(2,1)S(1)} %copy-done, bf16[1024,2048]{1,0:T(8,128)(2,1)} %own_ref.1), custom_call_target="tpu_custom_call" | custom-call | tf_op jit(solution)/shard_map/pallas_call | solution.py:345
  111.0 0.2 multiply_reduce_fusion
  111.3 0.0 copy-start.7
  111.3 23.7 %psum.7 = f32[256]{0:T(256)S(1)} all-reduce(f32[256]{0:T(256)S(1)} %multiply_reduce_fusion), channel_id=1, replica_groups=mesh['groups'=2,'ctx'=4,'tp'=4] {'tp'}, use_global_device_ids=true, to_apply=%region_1.0 | all-reduce | flops 256 | bytes 2048 | tf_op jit(solution)/shard_map/psum | solution.py:658
  134.9 0.7 dynamic_slice.3
  135.6 0.2 multiply_convert_fusion
  135.9 1.3 collective-permute-start
  137.2 1.3 collective-permute-start.1
  139.2 0.0 copy-done.6
  139.2 0.0 copy-done.7
  139.2 0.0 copy-start.2
  139.2 0.0 copy-start.3
  139.3 0.0 collective-permute-done
  139.3 16.0 %collective-permute-done.1 = bf16[16,2048]{1,0:T(8,128)(2,1)S(1)} collective-permute-done((bf16[16,2048]{1,0:T(8,128)(2,1)S(1)}, bf16[16,2048]{1,0:T(8,128)(2,1)S(1)}, u32[]{:S(2)}, u32[]{:S(2)}) %collective-permute-start.1) | collective-permute-done | bytes 65568 | tf_op jit(solution)/shard_map/ppermute | solution.py:27
  155.3 0.8 fusion.pooled_ref
  156.1 0.0 copy-done.2
  156.1 83.2 %shard_map.141 = (f32[768,768]{1,0:T(8,128)S(1)}, bf16[256,768]{1,0:T(8,128)(2,1)S(1)}) custom-call(bf16[256,2048]{1,0:T(8,128)(2,1)S(1)} %fusion.pooled_ref, bf16[2048,3072]{1,0:T(8,128)(2,1)} %proj_ref.1, bf16[256,768]{1,0:T(8,128)(2,1)S(1)} %copy-done.2, bf16[768,3072]{1,0:T(8,128)(2,1)} %so_ref.1, bf16[256,768]{1,0:T(8,128)(2,1)S(1)} %copy-done.3, ...), custom_call_target="tpu_custom_call" | custom-call | tf_op jit(solution)/shard_map/pallas_call | solution.py:611
  239.3 1.4 copy.18
  240.7 0.7 copy.19
  (10 shorter events, 0.1 us)
Async XLA Ops:
  0.6 1.2 copy-start
  1.9 1.0 copy-start.1
  2.9 0.9 copy-start.4
  3.8 0.9 copy-start.5
  111.2 27.9 %copy-start.6 = (s32[256]{0:T(256)S(1)}, s32[256]{0:T(256)}, u32[]{:S(2)}) copy-start(s32[256]{0:T(256)} %param.21) | copy-start | bytes 3076
  111.3 28.0 %copy-start.7 = (s32[256]{0:T(256)S(1)}, s32[256]{0:T(256)}, u32[]{:S(2)}) copy-start(s32[256]{0:T(256)} %param.20) | copy-start | bytes 3076
  135.9 3.4 %collective-permute-start = (bf16[16,2048]{1,0:T(8,128)(2,1)S(1)}, bf16[16,2048]{1,0:T(8,128)(2,1)S(1)}, u32[]{:S(2)}, u32[]{:S(2)}) collective-permute-start(bf16[16,2048]{1,0:T(8,128)(2,1)S(1)} %get-tuple-element.2), channel_id=1, source_target_pairs={{0,4},{4,8},{8,12},{1,5},{5,9},{9,13},{2,6},{6,10},{10,14},{3,7},{... | collective-permute-start | bytes 196616 | tf_op jit(solution)/shard_map/ppermute | solution.py:25
  137.2 18.1 %collective-permute-start.1 = (bf16[16,2048]{1,0:T(8,128)(2,1)S(1)}, bf16[16,2048]{1,0:T(8,128)(2,1)S(1)}, u32[]{:S(2)}, u32[]{:S(2)}) collective-permute-start(bf16[16,2048]{1,0:T(8,128)(2,1)S(1)} %get-tuple-element.3), channel_id=1, source_target_pairs={{4,0},{8,4},{12,8},{5,1},{9,5},{13,9},{6,2},{10,6},{14,10},{7,3},{... | collective-permute-start | bytes 196616 | tf_op jit(solution)/shard_map/ppermute | solution.py:27
  139.2 16.8 %copy-start.2 = (bf16[256,768]{1,0:T(8,128)(2,1)S(1)}, bf16[256,768]{1,0:T(8,128)(2,1)}, u32[]{:S(2)}) copy-start(bf16[256,768]{1,0:T(8,128)(2,1)} %sc_ref.1) | copy-start | bytes 1179652
  139.2 16.8 %copy-start.3 = (bf16[256,768]{1,0:T(8,128)(2,1)S(1)}, bf16[256,768]{1,0:T(8,128)(2,1)}, u32[]{:S(2)}) copy-start(bf16[256,768]{1,0:T(8,128)(2,1)} %res_ref.3) | copy-start | bytes 1179652
